TPU v7x, 128 devices: a whole 4x4x4 slice. The times are simulated.
128 devices in a mesh: seg: 8 (over y, core), freq: 4 (over z), blk: 4 (over x).
Axes of the slice: x: 4, y: 4, z: 4, core: 2. Of those that a mesh axis runs over, the one named last changes fastest.
Arguments:
- samples: bfloat16 [64, 4096, 2048], P(('seg', 'freq'), 'blk'), may hold values from -100 to 100, as said below
- valid_counts: int32 [32], P('blk'), may hold values from 16 to 128, as said below
- channel_mask: int32 [4096], P('blk'), may hold values 0 or 1
- block_pairs: int32 [16, 2], P('blk'), may hold values from 0 to 31, as said below
Outputs:
- stacked: bfloat16 [16, 1024, 2, 128, 128], P('blk', ('seg', 'freq'))
Inputs may be any that keep to these rules, and one draw needn't show every extreme that they name: A segment's samples are a scale of its own for each segment and channel times values of order one. `valid_counts`: some block has all 128 channels valid. `block_pairs`: the rows of one index d of blk name a first block in d * 8 to (d + 1) * 8 - 1 and a partner that is 0 to 4 blocks after it; on index 0 one row reaches 4.
All inputs are finite; a program needn't handle non-finite values. No bound on the sum of `channel_mask` on one device may be relied on, other than what follows from the above.
Results may differ from a plain program's by a relative error of at most 0.0064.
Values may be sent and summed in bfloat16 or wider, within the bound.
No kernel may reach another device: no remote copies, remote signals or barrier semaphores. Data moves between devices by JAX's collectives and lax.ppermute only.
A program may use at most 128 MiB of HBM per device.

v0:
```python
import math

import jax
import jax.numpy as jnp
from jax import lax
from jax.sharding import PartitionSpec as P

HB = 4


def passed_along(shard, axis, by):
    peers = lax.axis_size(axis)
    pairs = [(i, i + by) for i in range(peers) if 0 <= i + by < peers]
    return lax.ppermute(shard, axis, pairs)


def transform_table(bin_order, samples_len):
    times = jnp.arange(samples_len, dtype=jnp.int32)
    phase = bin_order[:, None] * times[None, :] % samples_len
    angle = phase.astype(jnp.float32) * (2.0 * math.pi / samples_len)
    taper = 0.5 - 0.5 * jnp.cos(times.astype(jnp.float32) * (2.0 * math.pi / samples_len))
    return jnp.stack([taper * jnp.cos(angle), -taper * jnp.sin(angle)], 1).astype(jnp.bfloat16)


def shards(samples, valid_counts, channel_mask, block_pairs):
    samples_len = samples.shape[2]
    channels_local = samples.shape[1]
    block_count = valid_counts.shape[0]
    width = channels_local // block_count
    bins_total = samples_len // 2
    natural_order = jnp.arange(bins_total, dtype=jnp.int32)
    table = transform_table(natural_order, samples_len)
    spectra = jnp.einsum("kqt,sct->kqsc", table, samples, preferred_element_type=jnp.float32)
    power_mean = jnp.sum(spectra * spectra, axis=(0, 1)) / bins_total
    within = jnp.arange(width, dtype=jnp.int32)[None, :] < valid_counts[:, None]
    channel_valid = (within.reshape(channels_local) & (channel_mask == 1)).astype(jnp.float32)
    whitened = (spectra * (lax.rsqrt(power_mean + 1e-06) * channel_valid)).astype(jnp.bfloat16)
    merged = lax.all_to_all(whitened, ("seg", "freq"), split_axis=0, concat_axis=2, tiled=True)
    local_bins, parts_count, segment_total = (merged.shape[0], merged.shape[1], merged.shape[2])
    blocks = merged.reshape(local_bins, parts_count, segment_total, block_count, width)
    rim_blocks = passed_along(blocks[:, :, :, :HB], "blk", -1)
    extended = jnp.concatenate([blocks, rim_blocks], 3)
    base_block = lax.axis_index("blk") * block_count
    first_local = block_pairs[:, 0] - base_block
    partner_local = block_pairs[:, 1] - base_block
    left_block = jnp.take(extended, first_local, axis=3)
    right_block = jnp.take(extended, partner_local, axis=3)
    left_real, left_imag = (left_block[:, 0], left_block[:, 1])
    right_real, right_imag = (right_block[:, 0], right_block[:, 1])
    cross_real = jnp.einsum(
        "kspc,kspd->pkcd", left_real, right_real, preferred_element_type=jnp.float32
    )
    cross_real = cross_real + jnp.einsum(
        "kspc,kspd->pkcd", left_imag, right_imag, preferred_element_type=jnp.float32
    )
    cross_imag = jnp.einsum(
        "kspc,kspd->pkcd", left_imag, right_real, preferred_element_type=jnp.float32
    )
    cross_imag = cross_imag - jnp.einsum(
        "kspc,kspd->pkcd", left_real, right_imag, preferred_element_type=jnp.float32
    )
    stack_scale = 1.0 / math.sqrt(segment_total)
    return (jnp.stack([cross_real, cross_imag], 2) * stack_scale).astype(jnp.bfloat16)


def solution(mesh):
    placed = (P(("seg", "freq"), "blk", None), P("blk"), P("blk"), P("blk", None))
    return jax.shard_map(
        shards,
        mesh=mesh,
        in_specs=placed,
        out_specs=P("blk", ("seg", "freq"), None, None, None),
        check_vma=False,
    )
```

profile of v0, /device:TPU:2, one launch (start us, length us, event | category | flops | bytes accessed | tf_op | source)
XLA Modules:
  0.0 371.8 jit_solution(14129057680249884880)
XLA Ops:
  0.0 0.0 copy-start.4
  0.0 0.1 fusion.18
  0.1 0.1 multiply_subtract_fusion
  0.1 35.0 %multiply_convert_fusion.1 = (bf16[1024,1,2048]{2,0,1:T(8,128)(2,1)S(1)}, bf16[1024,1,2048]{2,0,1:T(8,128)(2,1)}) fusion(f32[2048]{0:T(1024)S(1)} %fusion.18, f32[2048]{0:T(1024)S(1)} %multiply_subtract_fusion), kind=kLoop, calls=%fused_computation.19 | loop fusion | flops 37748736 | bytes 8404992 | tf_op jit(solution)/shard_map/convert.1
  35.1 0.0 copy-done.4
  35.1 0.0 copy-done.2
  35.1 0.1 fusion.17
  35.2 31.2 %multiply_reduce_fusion = (f32[2,1024]{1,0:T(2,128)S(1)}, f32[1024,2,2,1024]{3,0,2,1:T(8,128)S(1)}) fusion(bf16[2,1024,2048]{2,1,0:T(8,128)(2,1)} %param.6, bf16[1024,1,2048]{2,0,1:T(8,128)(2,1)S(1)} %get-tuple-element.14, bf16[1024,1,2048]{2,0,1:T(8,128)(2,1)} %get-tuple-element.15), kind=kOutput, calls=%fused_computation.5 | convolution fusion | flops 17205032960 | bytes 33562624 | tf_op jit(solution)/shard_map/kqt,sct->kqsc/dot_general | solution.py:33
  66.4 2.9 multiply_convert_fusion
  69.3 17.3 %copy.12 = bf16[1024,2,2,1024]{3,2,1,0:T(2,128)(2,1)S(1)} copy(bf16[1024,2,2,1024]{3,0,2,1:T(8,128)(2,1)S(1)} %multiply_convert_fusion) | data formatting | bytes 16777216 | tf_op jit(solution)/shard_map/convert_element_type | solution.py:37
  86.6 104.9 %all_to_all.15 = bf16[1024,2,2,1024]{3,2,1,0:T(2,128)(2,1)} all-to-all(bf16[1024,2,2,1024]{3,2,1,0:T(2,128)(2,1)S(1)} %copy.12), channel_id=1, replica_groups=mesh['seg'=8,'freq'=4,'blk'=4] {'seg','freq'}, dimensions={0} | all-to-all | bytes 16777216 | tf_op jit(solution)/shard_map/all_to_all | solution.py:38
  191.5 10.4 %copy.13 = bf16[32,32,2,2,1024]{4,1,3,0,2:T(8,128)(2,1)} copy(bf16[32,32,2,2,1024]{4,3,2,1,0:T(2,128)(2,1)} %bitcast.59) | data formatting | bytes 16777216 | tf_op jit(solution)/shard_map/all_to_all | solution.py:38
  201.9 8.8 %copy.20 = bf16[512,8,8,128]{3,2,1,0:T(8,128)(2,1)} copy(bf16[512,8,8,128]{3,1,2,0:T(8,128)(2,1)} %bitcast.60) | data formatting | bytes 16777216
  210.6 5.7 %slice.32 = bf16[32,2,64,4,128]{4,3,0,2,1:T(4,128)(2,1)S(1)} slice(bf16[32,2,64,8,128]{4,3,0,2,1:T(8,128)(2,1)} %bitcast.57), slice={[0:32], [0:2], [0:64], [0:4], [0:128]} | slice | bytes 8388608 | tf_op jit(solution)/shard_map/slice | solution.py:41
  216.3 4.7 %copy.28 = bf16[32,2,64,4,128]{4,2,1,0,3:T(8,128)(2,1)} copy(bf16[32,2,64,4,128]{4,3,0,2,1:T(4,128)(2,1)S(1)} %slice.32) | data formatting | bytes 8388608
  221.0 2.6 collective-permute-start
  223.6 0.0 copy-done.3
  223.7 12.0 %constant_dynamic-update-slice_fusion.1 = bf16[32,2,64,12,128]{4,2,1,0,3:T(8,128)(2,1)} fusion(bf16[32,2,64,8,128]{4,3,0,2,1:T(8,128)(2,1)} %bitcast.58), kind=kLoop, calls=%fused_computation.39 | loop fusion | bytes 16777216
  235.7 79.0 %collective-permute-done = bf16[32,2,64,4,128]{4,2,1,0,3:T(8,128)(2,1)} collective-permute-done((bf16[32,2,64,4,128]{4,2,1,0,3:T(8,128)(2,1)}, bf16[32,2,64,4,128]{4,2,1,0,3:T(8,128)(2,1)}, u32[]{:S(2)}, u32[]{:S(2)}) %collective-permute-start) | collective-permute-done | bytes 4194336 | tf_op jit(solution)/shard_map/ppermute | solution.py:14
  314.7 6.0 %constant_dynamic-update-slice_fusion = bf16[32,2,64,12,128]{4,2,1,0,3:T(8,128)(2,1)} fusion(bf16[32,2,64,12,128]{4,2,1,0,3:T(8,128)(2,1)} %constant_dynamic-update-slice_fusion.1, bf16[32,2,64,4,128]{4,2,1,0,3:T(8,128)(2,1)} %collective-permute-done), kind=kLoop, calls=%fused_computation.38 | loop fusion | bytes 8388608 | tf_op jit(solution)/shard_map/concatenate | solution.py:42
  320.7 7.6 %gather_fusion = bf16[4,32,2,64,128]{4,3,2,1,0:T(8,128)(2,1)} fusion(bf16[32,2,64,12,128]{4,2,1,0,3:T(8,128)(2,1)} %constant_dynamic-update-slice_fusion, s32[1024]{0:T(1024)S(1)} %get-tuple-element.17), kind=kCustom, calls=%fused_computation.clone | custom fusion | bytes 8388624 | tf_op jit(solution)/shard_map/jit(_take)/gather | solution.py:46
  328.3 7.7 %gather_fusion.1 = bf16[4,32,2,64,128]{4,3,2,1,0:T(8,128)(2,1)} fusion(bf16[32,2,64,12,128]{4,2,1,0,3:T(8,128)(2,1)} %constant_dynamic-update-slice_fusion, s32[1024]{0:T(1024)S(1)} %get-tuple-element.16), kind=kCustom, calls=%fused_computation.1.clone | custom fusion | bytes 8388624 | tf_op jit(solution)/shard_map/jit(_take)/gather | solution.py:47
  336.0 2.8 fusion.12
  338.8 0.6 copy-done.1
  339.4 0.5 fusion.11
  339.9 1.3 fusion.13
  341.2 1.3 fusion.14
  342.6 4.8 %add_bitcast_fusion = f32[4,32,1,128,128]{4,3,1,0,2:T(8,128)} fusion(f32[4,32,128,128]{3,2,1,0:T(8,128)S(1)} %fusion.13, bf16[32,2,64,4,128]{4,2,0,3,1:T(8,128)(2,1)S(1)} %fusion.12, bf16[32,2,64,4,128]{4,2,0,3,1:T(8,128)(2,1)S(1)} %fusion.11), kind=kOutput, calls=%fused_computation.18 | convolution fusion | flops 270532608 | bytes 20971520 | tf_op jit(solution)/shard_map/kspc,kspd->pkcd/dot_general | solution.py:53
  347.4 5.4 %subtract_bitcast_fusion = f32[4,32,1,128,128]{4,3,1,0,2:T(8,128)} fusion(f32[4,32,128,128]{3,2,1,0:T(8,128)S(1)} %fusion.14, bf16[32,2,64,4,128]{4,2,0,3,1:T(8,128)(2,1)S(1)} %fusion.12, bf16[32,2,64,4,128]{4,2,0,3,1:T(8,128)(2,1)S(1)} %fusion.11), kind=kOutput, calls=%fused_computation.17 | convolution fusion | flops 270532608 | bytes 20971520 | tf_op jit(solution)/shard_map/kspc,kspd->pkcd/dot_general | solution.py:59
  352.8 0.6 copy-done
  353.3 7.7 %fusion = bf16[4,32,2,128,128]{4,3,1,0,2:T(8,128)(2,1)} fusion(f32[4,32,1,128,128]{4,3,1,0,2:T(8,128)} %subtract_bitcast_fusion, f32[4,32,1,128,128]{4,3,1,0,2:T(8,128)S(1)} %copy-done), kind=kLoop, calls=%fused_computation.3 | loop fusion | flops 12582912 | bytes 25165824 | tf_op jit(solution)/shard_map/convert_element_type | solution.py:63
  361.1 10.5 %copy.18 = bf16[4,32,2,128,128]{4,3,2,1,0:T(8,128)(2,1)} copy(bf16[4,32,2,128,128]{4,3,1,0,2:T(8,128)(2,1)} %fusion) | data formatting | bytes 16777216 | tf_op jit(solution)/shard_map/convert_element_type | solution.py:63
  (7 shorter events, 0.0 us)
Async XLA Ops:
  0.0 35.1 %copy-start.4 = (s32[8]{0:T(128)S(1)}, s32[8]{0:T(128)}, u32[]{:S(2)}) copy-start(s32[8]{0:T(128)} %param.7) | copy-start | bytes 100
  0.0 35.1 %copy-start.2 = (s32[1024]{0:T(1024)S(1)}, s32[1024]{0:T(1024)}, u32[]{:S(2)}) copy-start(s32[1024]{0:T(1024)} %param.8) | copy-start | bytes 12292
  210.6 13.0 %copy-start.3 = (s32[4,2]{0,1:T(2,128)S(1)}, s32[4,2]{0,1:T(2,128)}, u32[]{:S(2)}) copy-start(s32[4,2]{0,1:T(2,128)} %param.9) | copy-start | bytes 100
  221.0 93.7 %collective-permute-start = (bf16[32,2,64,4,128]{4,2,1,0,3:T(8,128)(2,1)}, bf16[32,2,64,4,128]{4,2,1,0,3:T(8,128)(2,1)}, u32[]{:S(2)}, u32[]{:S(2)}) collective-permute-start(bf16[32,2,64,4,128]{4,2,1,0,3:T(8,128)(2,1)} %copy.28), channel_id=1, source_target_pairs={{1,0},{2,1},{3,2},{5,4},{6,5},{7,6},{9,8},{10,9},{11,10},{13,12},{... | collective-permute-start | bytes 12582920 | tf_op jit(solution)/shard_map/ppermute | solution.py:14
  336.0 3.4 copy-start.1
  347.4 6.0 %copy-start = (f32[4,32,1,128,128]{4,3,1,0,2:T(8,128)S(1)}, f32[4,32,1,128,128]{4,3,1,0,2:T(8,128)}, u32[]{:S(2)}) copy-start(f32[4,32,1,128,128]{4,3,1,0,2:T(8,128)} %add_bitcast_fusion) | copy-start | bytes 25165828
where the time goes:
time: 379 us; the launch traced here: 372 us
  blocking collectives  105 us (28%)
  local copies, waits for them, and re-layouts  91.8 us (24%)
  waiting for transfers between devices  79 us (21%)
  other arithmetic  49.1 us (13%)
  matrix products  44 us (12%)
    all_to_all x1, blocking collectives, shards(): lax.all_to_all(whitened, ('seg', 'freq'), split_axis=0, concat_axis=2, ti...  105 us
    ppermute x1, waiting for transfers between devices, passed_along(): return lax.ppermute(shard, axis, pairs)  79 us
    another operation x1, other arithmetic  35 us
    dot_general x1, matrix products, shards(): jnp.einsum('kqt,sct->kqsc', table, samples, preferred_element_type=jnp.fl...  31.2 us
    unnamed x13, local copies, waits for them, and re-layouts  26.7 us
    convert_element_type x1, local copies, waits for them, and re-layouts, shards(): (spectra * (lax.rsqrt(power_mean + 1e-06) * channel_valid)).astype(jnp.bf...  17.3 us
    convert_element_type x1, local copies, waits for them, and re-layouts, shards(): (jnp.stack([cross_real, cross_imag], 2) * stack_scale).astype(jnp.bfloat16)  10.5 us
    all_to_all x1, local copies, waits for them, and re-layouts, shards(): lax.all_to_all(whitened, ('seg', 'freq'), split_axis=0, concat_axis=2, ti...  10.4 us
  transfers between devices with their start and end apart: 1, of which 1 were waited for; matrix products, arithmetic and copies ran while one was open for 3% of the time, Pallas kernels for 0%

commit v1 on v0

v1 whole, which is shorter than its diff:
```python
import math

import jax
import jax.numpy as jnp
import numpy as np
from jax import lax
from jax.experimental import pallas as pl
from jax.experimental.pallas import tpu as pltpu
from jax.sharding import PartitionSpec as P

WIDTH = 128
HB = 4
SIZES = ((128, 320), (192, 320), (256, 384), (320, 448), (512, 512))
VMEM = 60 * 1024 * 1024
NEXT = 1 << 16


def transform_table(bins, samples_len):
    times = np.arange(samples_len, dtype=np.int64)
    order = np.arange(bins, dtype=np.int64)
    phase = (order[:, None] * times[None, :]) % samples_len
    angle = phase * (2.0 * math.pi / samples_len)
    taper = 0.5 - 0.5 * np.cos(times * (2.0 * math.pi / samples_len))
    table = np.stack([taper * np.cos(angle), -taper * np.sin(angle)], 1)
    return table.reshape(2 * bins, samples_len).astype(np.float32).astype(jnp.bfloat16)


def regroup_matrix():
    out = np.zeros((256, 256), np.float32)
    for src in range(16):
        for row in range(16):
            out[row * 16 + src, src * 16 + row] = 1.0
    return out.astype(jnp.bfloat16)


def whole_tiles(count):
    return (count + WIDTH - 1) // WIDTH * WIDTH


def plan_kernel(block_count, me_ref, own_ref, n1_ref, n2_ref, n3_ref, place_ref, where_ref, info_ref):
    refs = (own_ref, n1_ref, n2_ref, n3_ref)
    planes = len(refs)
    me = me_ref[0, 0]
    pairs = where_ref.shape[0] // 2
    firsts = [ref[block_count : block_count + 1, :pairs] for ref in refs]
    partners = [ref[block_count + 1 : block_count + 2, :pairs] for ref in refs]
    flat = lambda x: x.astype(jnp.float32).astype(jnp.bfloat16)
    upto = flat(
        (lax.broadcasted_iota(jnp.int32, (WIDTH, WIDTH), 0) <= lax.broadcasted_iota(jnp.int32, (WIDTH, WIDTH), 1)).astype(jnp.int32)
    )
    row_of = lax.broadcasted_iota(jnp.int32, (block_count, 1), 0)

    def flags(j):
        ids = row_of + lax.rem(me + j, planes) * block_count
        named = jnp.zeros((block_count, 1), jnp.int32)
        rim = jnp.zeros((block_count, 1), jnp.int32)
        for first, partner in zip(firsts, partners):
            hit = partner == ids
            crosses = (first // block_count) != (partner // block_count)
            named = named + jnp.sum((hit | (first == ids)).astype(jnp.int32), axis=1, keepdims=True)
            rim = rim + jnp.sum((hit & crosses).astype(jnp.int32), axis=1, keepdims=True)
        return ids, named > 0, rim > 0

    def ranks(chosen):
        inside = jnp.dot(flat(chosen), upto, preferred_element_type=jnp.float32)
        sums = inside[:, WIDTH - 1 :]
        before = jnp.zeros((block_count, 1), jnp.float32)
        for b in range(block_count - 1):
            before = before + jnp.where(row_of > b, sums[b : b + 1], 0.0)
        return (inside + before).astype(jnp.int32) - 1, jnp.sum(sums, axis=0, keepdims=True).astype(jnp.int32)

    rim_most = jnp.zeros((1, 1), jnp.int32)
    all_list, low_list = [], []
    for j in range(planes):
        ids, named, rim = flags(j)
        valid = refs[j][:block_count]
        counts = jnp.sum(valid, axis=1, keepdims=True)
        total = lambda m: jnp.sum(jnp.where(m, counts, 0), axis=0, keepdims=True)
        rim_most = jnp.maximum(rim_most, total(rim))
        all_list.append(total(named))
        low_list.append(total(named & (row_of < HB)))
        if j == 0:
            own_ids = ids
            rim_mask = jnp.where(rim, valid, 0)
            rest_mask = jnp.where(named & jnp.logical_not(rim), valid, 0)
            rim_rank, rim_count = ranks(rim_mask)
            rest_rank, _ = ranks(rest_mask)
            place = jnp.where(rim_mask > 0, rim_rank, jnp.where(rest_mask > 0, rest_rank + rim_count, -1))
        if j == 1:
            next_ids = ids
            next_mask = jnp.where(rim, valid, 0)
            next_rank, _ = ranks(next_mask)
            next_place = jnp.where(next_mask > 0, next_rank + NEXT, -1)
    branch = jnp.zeros((1, 1), jnp.int32) + (len(SIZES) - 1)
    for n in reversed(range(len(SIZES) - 1)):
        r, l = SIZES[n]
        fits = rim_most <= r
        for everything, low in zip(all_list, low_list):
            fits = fits & (everything - jnp.minimum(low, r) <= l)
        branch = jnp.where(fits, n, branch)
    size = jnp.zeros((1, 1), jnp.int32)
    for n, (r, _) in enumerate(SIZES):
        size = jnp.where(branch == n, r, size)
    behind = jnp.where(row_of >= HB, jnp.maximum(size - low_list[0], 0), 0)
    place = jnp.where(place >= 0, place + behind + whole_tiles(size) - size, -1)
    place_ref[...] = place

    def look(block):
        here = jnp.max(jnp.where(own_ids == block, place, -1), axis=0, keepdims=True)
        beyond = jnp.max(jnp.where(next_ids == block, next_place, -1), axis=0, keepdims=True)
        return jnp.maximum(here, beyond)

    found = [look(firsts[0][:, p : p + 1]) for p in range(pairs)] + [look(partners[0][:, p : p + 1]) for p in range(pairs)]
    found = jnp.concatenate(found, 0)
    where_ref[...] = found
    starts = jnp.min(jnp.where(found >= 0, found, 2 * NEXT), axis=1, keepdims=True)
    starts = jnp.where(starts == 2 * NEXT, 0, starts)
    lanes = lax.broadcasted_iota(jnp.int32, info_ref.shape, 1)
    info_ref[...] = jnp.where(lanes == 0, starts, branch)


def plan(me, own, others, block_count, pairs):
    vmem = pl.BlockSpec(memory_space=pltpu.VMEM)
    return pl.pallas_call(
        lambda *refs: plan_kernel(block_count, *refs),
        in_specs=[pl.BlockSpec(memory_space=pltpu.SMEM)] + [vmem] * 4,
        out_specs=[vmem] * 3,
        out_shape=[
            jax.ShapeDtypeStruct((block_count, WIDTH), jnp.int32),
            jax.ShapeDtypeStruct((2 * pairs, WIDTH), jnp.int32),
            jax.ShapeDtypeStruct((2 * pairs, WIDTH), jnp.int32),
        ],
    )(me, own, *others)


def spectra_kernel(base, count, tile, across, place_ref, samples_ref, table_ref, out_ref, held, table, picked, spectra, power, held_sem, table_sem):
    segs, channels, samples_len = held.shape
    lanes = picked.shape[0]
    pieces = table_sem.shape[0]
    rows = table.shape[0] // pieces

    get = [pltpu.make_async_copy(samples_ref.at[s, :channels, :], held.at[s], held_sem.at[s]) for s in range(segs)]
    for copy in get:
        copy.start()

    def table_copy(n):
        here = pl.ds(pl.multiple_of(n * rows, rows), rows)
        return pltpu.make_async_copy(table_ref.at[here, :], table.at[here, :], table_sem.at[n])

    @pl.loop(0, pieces)
    def _(n):
        table_copy(n).start()

    target = lax.broadcasted_iota(jnp.int32, (count, channels), 0) + base
    chosen = (place_ref[:, :channels] == target).astype(jnp.bfloat16)
    for s in range(segs):
        get[s].wait()

        @pl.loop(0, samples_len // tile)
        def _(n):
            cols = pl.ds(pl.multiple_of(n * tile, tile), tile)
            found = jnp.dot(chosen, held[s, :, cols], preferred_element_type=jnp.float32)
            picked[s * count : (s + 1) * count, cols] = found.astype(jnp.bfloat16)

    power[...] = jnp.zeros(power.shape, jnp.float32)

    @pl.loop(0, pieces)
    def _(n):
        here = pl.ds(pl.multiple_of(n * rows, rows), rows)
        table_copy(n).wait()

        @pl.loop(0, lanes // across)
        def _(m):
            cols = pl.ds(pl.multiple_of(m * across, across), across)
            block = lax.dot_general(
                table[here, :], picked[cols, :], (((1,), (1,)), ((), ())), preferred_element_type=jnp.float32
            )
            spectra[here, cols] = block
            power[:, cols] = power[:, cols] + jnp.sum((block * block).reshape(rows // 8, 8, across), axis=0)

    scale = lax.rsqrt(jnp.sum(power[...], axis=0, keepdims=True) / (table.shape[0] // 2) + 1e-06)
    peers, each, _ = out_ref.shape

    @pl.loop(0, peers)
    def _(peer):
        here = pl.ds(pl.multiple_of(peer * each, each), each)
        out_ref[peer] = (spectra[here, : segs * count] * scale[:, : segs * count]).astype(jnp.bfloat16)


def spectra_chunk(samples, table, place, channels, base, count, peers, urgent):
    segs, _, samples_len = samples.shape
    rows_total = table.shape[0]
    lanes = segs * count
    pieces, tile, across = (4, 512, lanes) if urgent else (4, 256, 256)
    wide = (lanes + across - 1) // across * across
    body = lambda *refs: spectra_kernel(base, count, tile, across, *refs)
    hbm = pl.BlockSpec(memory_space=pl.ANY)
    vmem = pl.BlockSpec(memory_space=pltpu.VMEM)
    return pl.pallas_call(
        body,
        in_specs=[vmem, hbm, hbm],
        out_specs=vmem,
        out_shape=jax.ShapeDtypeStruct((peers, rows_total // peers, lanes), jnp.bfloat16),
        scratch_shapes=[
            pltpu.VMEM((segs, channels, samples_len), jnp.bfloat16),
            pltpu.VMEM((rows_total, samples_len), jnp.bfloat16),
            pltpu.VMEM((wide, samples_len), jnp.bfloat16),
            pltpu.VMEM((rows_total, wide), jnp.float32),
            pltpu.VMEM((8, wide), jnp.float32),
            pltpu.SemaphoreType.DMA((segs,)),
            pltpu.SemaphoreType.DMA((pieces,)),
        ],
        compiler_params=pltpu.CompilerParams(vmem_limit_bytes=VMEM + 7 * 512 * 1024),
        cost_estimate=pl.CostEstimate(
            flops=2 * segs * count * samples_len * (rows_total + channels),
            bytes_accessed=2 * (segs * channels * samples_len + rows_total * samples_len),
            transcendentals=0,
        ),
    )(place, samples, table)


def stack_kernel(counts, scale, info_ref, where_ref, regroup_ref, xr_ref, xl_ref, zr_ref, out_ref, pick_l, pick_r, held):
    r_count, l_count = counts
    own = whole_tiles(r_count) + whole_tiles(l_count)
    pairs, bins, _, width, _ = out_ref.shape
    window = 2 * width
    behind = own + whole_tiles(r_count) - r_count - NEXT

    def start(n):
        first = info_ref[n, 0]
        first = jnp.where(first >= NEXT, first + behind, first)
        return pl.multiple_of((first // width) * width, width)

    @pl.when(pl.program_id(0) == 0)
    def _():
        held[:, held.shape[1] - width :] = jnp.zeros((held.shape[0], width), held.dtype)
        where = where_ref[...]
        where = jnp.where(where >= NEXT, where + behind, where)
        eye = lax.broadcasted_iota(jnp.int32, (width, width), 0) == lax.broadcasted_iota(jnp.int32, (width, width), 1)
        for p in range(pairs):
            pick_l[p] = (where[p : p + 1] == lax.broadcasted_iota(jnp.int32, (window, width), 0) + start(p)).astype(jnp.bfloat16) * jnp.bfloat16(scale)
            row = where[pairs + p : pairs + p + 1]
            pick_r[p] = (row == lax.broadcasted_iota(jnp.int32, (window, width), 0) + start(pairs + p)).astype(jnp.bfloat16)

    chunks = ((xr_ref, r_count, 0, True), (xl_ref, l_count, whole_tiles(r_count), False), (zr_ref, r_count, own, True))
    for ref, count, at, to_end in chunks:
        full = whole_tiles(count)
        for h in range(2):
            rows = ref[h * 16 : (h + 1) * 16].reshape(256, 2 * count)
            rows = jnp.dot(regroup_ref[...], rows, preferred_element_type=jnp.float32)
            by_seg = [rows[:, :full], rows[:, 2 * count - full :]]
            if full != count:
                turn = 0 if to_end else 1
                by_seg[turn] = pltpu.roll(by_seg[turn], WIDTH // 2 if to_end else full - WIDTH // 2, 1)
            for s in range(2):
                part = by_seg[s].astype(jnp.bfloat16)
                for k in range(bins):
                    to = k * 128 + (s * 2 + h) * 32
                    held[to : to + 32, at : at + full] = part[k * 32 : (k + 1) * 32]

    def one_pair(p):
        from_l = held[:, pl.ds(start(p), window)]
        left = jnp.dot(from_l, pick_l[p], preferred_element_type=jnp.float32)
        left = left.astype(jnp.bfloat16)
        from_r = held[:, pl.ds(start(pairs + p), window)]
        right = jnp.dot(from_r, pick_r[p], preferred_element_type=jnp.float32).astype(jnp.bfloat16)
        for k in range(bins):
            b = right[k * 128 : (k + 1) * 128]
            turned = []
            for g in range(4):
                turned.append(-b[g * 32 + 16 : g * 32 + 32])
                turned.append(b[g * 32 : g * 32 + 16])
            both = jnp.concatenate([b, jnp.concatenate(turned, 0)], 1)
            a = left[k * 128 : (k + 1) * 128]
            res = (lax.dot_general(a, both, (((0,), (0,)), ((), ())), preferred_element_type=jnp.float32)).astype(jnp.bfloat16)
            out_ref[p, k, 0] = res[:, :width]
            out_ref[p, k, 1] = res[:, width:]

    pl.loop(0, pairs, unroll=2 if r_count < 512 else 1)(one_pair)


def stacked_products(xr, xl, zr, info, where, regroup, pairs, scale):
    peers, rows, r_two = xr.shape
    l_two = xl.shape[2]
    r_count, l_count = r_two // 2, l_two // 2
    bins = rows // 2
    group = 8
    body = lambda *refs: stack_kernel((r_count, l_count), scale, *refs)
    whole = lambda shape: pl.BlockSpec(shape, lambda g: (0,) * len(shape))
    part = lambda lanes: pl.BlockSpec((peers, 2 * group, lanes), lambda g: (0, g, 0))
    return pl.pallas_call(
        body,
        grid=(bins // group,),
        in_specs=[
            pl.BlockSpec(memory_space=pltpu.SMEM), whole(where.shape), whole((256, 256)),
            part(r_two), part(l_two), part(r_two),
        ],
        out_specs=pl.BlockSpec((pairs, group, 2, WIDTH, WIDTH), lambda g: (0, g, 0, 0, 0)),
        out_shape=jax.ShapeDtypeStruct((pairs, bins, 2, WIDTH, WIDTH), jnp.bfloat16),
        scratch_shapes=[
            pltpu.VMEM((pairs, 2 * WIDTH, WIDTH), jnp.bfloat16),
            pltpu.VMEM((pairs, 2 * WIDTH, WIDTH), jnp.bfloat16),
            pltpu.VMEM((group * 128, 2 * whole_tiles(r_count) + whole_tiles(l_count) + WIDTH), jnp.bfloat16),
        ],
        compiler_params=pltpu.CompilerParams(vmem_limit_bytes=VMEM),
        cost_estimate=pl.CostEstimate(
            flops=2 * peers * rows * 2 * WIDTH * (4 * pairs * WIDTH + 2 * r_two + l_two),
            bytes_accessed=2 * (peers * rows * (2 * r_two + l_two) + pairs * bins * 2 * WIDTH * WIDTH),
            transcendentals=0,
        ),
    )(info, where, regroup, xr, xl, zr)


def shards(samples, valid_counts, channel_mask, block_pairs):
    segs, channels, samples_len = samples.shape
    block_count = valid_counts.shape[0]
    planes = lax.axis_size("blk")
    peers = lax.axis_size("seg") * lax.axis_size("freq")
    pairs = block_pairs.shape[0]
    bins = samples_len // 2

    table, regroup = lax.optimization_barrier(
        (jnp.asarray(transform_table(bins, samples_len)), jnp.asarray(regroup_matrix()))
    )
    within = jnp.arange(WIDTH, dtype=jnp.int32)[None, :] < valid_counts[:, None]
    valid = (within & (channel_mask.reshape(block_count, WIDTH) == 1)).astype(jnp.int32)
    lines = jnp.pad(block_pairs.T, ((0, block_count - 2), (0, WIDTH - pairs)))
    own = jnp.concatenate([valid, lines], 0)
    others = [
        lax.ppermute(own, "blk", [(i, (i - shift) % planes) for i in range(planes)]) for shift in range(1, planes)
    ]
    me = lax.axis_index("blk").astype(jnp.int32).reshape(1, 1)
    place, where, info = plan(me, own, others, block_count, pairs)
    place_row = place.reshape(1, channels)
    scale = 1.0 / math.sqrt(peers * segs)

    def with_sizes(r_count, l_count):
        def run(samples, table, regroup, place_row, where, info):
            own_r = spectra_chunk(samples, table, place_row, HB * WIDTH, whole_tiles(r_count) - r_count, r_count, peers, r_count < 512)
            xr = lax.all_to_all(own_r, ("seg", "freq"), split_axis=0, concat_axis=0, tiled=True)
            own_l = spectra_chunk(samples, table, place_row, channels, whole_tiles(r_count), l_count, peers, False)
            xr, own_l = lax.optimization_barrier((xr, own_l))
            zr = lax.ppermute(xr, "blk", [(i, i - 1) for i in range(1, planes)])
            xl = lax.all_to_all(own_l, ("seg", "freq"), split_axis=0, concat_axis=0, tiled=True)
            return stacked_products(xr, xl, zr, info, where, regroup, pairs, scale)

        return run

    return lax.switch(
        info[0, 1],
        [with_sizes(r, l) for r, l in SIZES],
        samples, table, regroup, place_row, where, info,
    )


def solution(mesh):
    placed = (P(("seg", "freq"), "blk", None), P("blk"), P("blk"), P("blk", None))
    return jax.shard_map(
        shards,
        mesh=mesh,
        in_specs=placed,
        out_specs=P("blk", ("seg", "freq"), None, None, None),
        check_vma=False,
    )
```

time: 379 us -> 113 us (0.30); the launches traced: 372 us -> 111 us
  blocking collectives: 105 us -> 0 us
  local copies, waits for them, and re-layouts: 91.8 us -> 2.66 us
  other arithmetic: 49.1 us -> 1.44 us
  Pallas kernels: 0 us -> 44.8 us
  matrix products: 44 us -> 0 us
  waiting for transfers between devices: 79 us -> 40.7 us
  starting transfers between devices: 2.59 us -> 20.9 us
    all_to_all x1 -> x0, blocking collectives: 105 us -> none  [shards(): lax.all_to_all(whitened, ('seg', 'freq'), split_axis=0, concat_axis=2, ti...]
    pallas_call x0 -> x4, Pallas kernels: none -> 44.8 us  [the longest x2 29.4 us: spectra_chunk(): pl.pallas_call(body, in_specs=[vmem, hbm, hbm], out_specs=vmem, out_shape...]
    dot_general x5 -> x0, matrix products: 44 us -> none  [the longest x1 31.2 us: shards(): jnp.einsum('kqt,sct->kqsc', table, samples, preferred_element_type=jnp.fl...]
    ppermute x1 -> x4, waiting for transfers between devices: 79 us -> 36.9 us  [the longest x1 35 us: run(): zr = lax.ppermute(xr, 'blk', [(i, i - 1) for i in range(1, planes)])]
    another operation x1 -> x0, other arithmetic: 35 us -> none
    convert_element_type x2 -> x0, local copies, waits for them, and re-layouts: 27.8 us -> none  [the longest x1 17.3 us: shards(): (spectra * (lax.rsqrt(power_mean + 1e-06) * channel_valid)).astype(jnp.bf...]
    unnamed x13 -> x8, local copies, waits for them, and re-layouts: 26.7 us -> 0.59 us
    gather x2 -> x0, local copies, waits for them, and re-layouts: 15.3 us -> none  [the longest x1 7.67 us: shards(): right_block = jnp.take(extended, partner_local, axis=3)]
  transfers between devices with their start and end apart: 1 -> 6, of which waited for: 1 -> 3; matrix products, arithmetic and copies ran while one was open for 3% -> 0% of each run, Pallas kernels for 0% -> 17%
where the time goes in v1:
time: 113 us; the launch traced here: 111 us
  Pallas kernels  44.8 us (40%)
  waiting for transfers between devices  40.7 us (36%)
  starting transfers between devices  20.9 us (18%)
  local copies, waits for them, and re-layouts  2.66 us (2%)
  other arithmetic  1.44 us (1%)
    ppermute x1, waiting for transfers between devices, run(): zr = lax.ppermute(xr, 'blk', [(i, i - 1) for i in range(1, planes)])  35 us
    pallas_call x2, Pallas kernels, spectra_chunk(): pl.pallas_call(body, in_specs=[vmem, hbm, hbm], out_specs=vmem, out_shape...  29.4 us
    pallas_call x1, Pallas kernels, stacked_products(): pl.pallas_call(body, grid=(bins // group,), in_specs=[pl.BlockSpec(memory...  14.2 us
    all_to_all x1, starting transfers between devices, run(): lax.all_to_all(own_r, ('seg', 'freq'), split_axis=0, concat_axis=0, tiled...  8.46 us
    ppermute x3, starting transfers between devices, shards(): lax.ppermute(own, 'blk', [(i, (i - shift) % planes) for i in range(planes)])  4.76 us
    all_to_all x1, starting transfers between devices, run(): lax.all_to_all(own_l, ('seg', 'freq'), split_axis=0, concat_axis=0, tiled...  4.06 us
    all_to_all x1, waiting for transfers between devices, run(): lax.all_to_all(own_r, ('seg', 'freq'), split_axis=0, concat_axis=0, tiled...  3.8 us
    ppermute x1, starting transfers between devices, run(): zr = lax.ppermute(xr, 'blk', [(i, i - 1) for i in range(1, planes)])  3.66 us
  transfers between devices with their start and end apart: 6, of which 3 were waited for; matrix products, arithmetic and copies ran while one was open for 0% of the time, Pallas kernels for 17%

profile of v1, /device:TPU:2, one launch (start us, length us, event | category | flops | bytes accessed | tf_op | source)
XLA Modules:
  0.0 111.3 jit_solution(14145290753939873578)
XLA Ops:
  0.0 0.8 fusion.1
  0.8 0.7 pad_add_fusion.refs_1_
  1.4 0.0 copy-start.9
  1.4 1.5 %collective-permute-start.7 = (s32[16,128]{1,0:T(8,128)S(1)}, s32[16,128]{1,0:T(8,128)S(1)}, u32[]{:S(2)}, u32[]{:S(2)}) collective-permute-start(s32[16,128]{1,0:T(8,128)S(1)} %pad_add_fusion.refs_1_), channel_id=1, source_target_pairs={{0,1},{1,2},{2,3},{3,0},{4,5},{5,6},{6,7},{7,4},{8,9},{9,10},{10,1... | collective-permute-start | bytes 24584 | tf_op jit(solution)/shard_map/ppermute | solution.py:330
  2.9 1.0 collective-permute-start.6
  4.0 2.2 %collective-permute-start.5 = (s32[16,128]{1,0:T(8,128)S(1)}, s32[16,128]{1,0:T(8,128)S(1)}, u32[]{:S(2)}, u32[]{:S(2)}) collective-permute-start(s32[16,128]{1,0:T(8,128)S(1)} %pad_add_fusion.refs_1_), channel_id=1, source_target_pairs={{0,3},{1,0},{2,1},{3,2},{4,7},{5,4},{6,5},{7,6},{8,11},{9,8},{10,9... | collective-permute-start | bytes 24584 | tf_op jit(solution)/shard_map/ppermute | solution.py:330
  6.2 0.0 collective-permute-done.7.refs_4_
  6.2 0.0 copy-start.10
  6.2 1.9 %collective-permute-done.6.refs_3_ = s32[16,128]{1,0:T(8,128)S(1)} collective-permute-done((s32[16,128]{1,0:T(8,128)S(1)}, s32[16,128]{1,0:T(8,128)S(1)}, u32[]{:S(2)}, u32[]{:S(2)}) %collective-permute-start.6) | collective-permute-done | bytes 8224 | tf_op jit(solution)/shard_map/ppermute | solution.py:330
  8.1 0.0 copy-start.11
  8.1 0.0 collective-permute-done.5.refs_2_
  8.1 0.0 copy-start.12
  8.1 0.0 copy-done.9
  8.1 0.0 copy-done.10
  8.1 0.6 copy-done.11
  8.7 0.0 copy-done.12
  8.7 1.3 %shard_map.69 = (s32[8,128]{1,0:T(8,128)S(1)}, s32[8,128]{1,0:T(8,128)S(1)}, s32[8,128]{1,0:T(8,128)S(1)}) custom-call(s32[1,1]{1,0:T(1,128)} %bitcast.refs_0_, s32[16,128]{1,0:T(8,128)} %copy-done.9, s32[16,128]{1,0:T(8,128)} %copy-done.12, s32[16,128]{1,0:T(8,128)} %copy-done.11, s32[16,128]{1,0:T(8,128)} %copy-done.10), custom_call_target="tpu_custom_call" | custom-call | tf_op jit(solution)/shard_map/pallas_call | solution.py:124
  10.0 0.6 slice.3
  11.2 100.1 %conditional.1 = (bf16[4,32,2,128,128]{4,3,2,1,0:T(8,128)(2,1)}) conditional(s32[]{:T(128)} %bitcast.3, (s32[1,1024]{1,0:T(1,128)S(1)}, bf16[2,1024,2048]{2,1,0:T(8,128)(2,1)}, bf16[2048,2048]{1,0:T(8,128)(2,1)}, s32[8,128]{1,0:T(8,128)S(1)}, s32[8,128]{1,0:T(8,128)S(1)}, ...), branch_computations={%region_0.1_spmd, %region_1.2_spmd, %region_2.3_spmd, %region_3.4_... | conditional | flops 28991029248 | bytes 88604776 | solution.py:349
  11.2 10.5 %branch_1_fun.3 = bf16[32,64,384]{2,1,0:T(8,128)(2,1)} custom-call(s32[1,1024]{1,0:T(1,128)S(1)} %get-tuple-element.82.refs_0_, bf16[2,1024,2048]{2,1,0:T(8,128)(2,1)} %get-tuple-element.83.refs_1_, bf16[2048,2048]{1,0:T(8,128)(2,1)} %get-tuple-element.84.refs_2_), custom_call_target="tpu_custom_call" | custom-call | flops 4026531840 | bytes 12582912 | tf_op jit(solution)/shard_map/cond/branch_1_fun/pallas_call | solution.py:199
  21.7 8.5 %all-to-all-start.2 = ((bf16[32,64,384]{2,1,0:T(8,128)(2,1)}), bf16[32,64,384]{2,1,0:T(8,128)(2,1)}, u32[]{:S(2)}, u32[]{:S(2)}) async-start(bf16[32,64,384]{2,1,0:T(8,128)(2,1)} %branch_1_fun.3), calls=%async_computation.2 | async-start | bytes 3145728 | tf_op jit(solution)/shard_map/cond/branch_1_fun/all_to_all | solution.py:340
  30.2 18.9 %branch_1_fun.4 = bf16[32,64,640]{2,1,0:T(8,128)(2,1)} custom-call(s32[1,1024]{1,0:T(1,128)S(1)} %get-tuple-element.82.refs_0_, bf16[2,1024,2048]{2,1,0:T(8,128)(2,1)} %get-tuple-element.83.refs_1_, bf16[2048,2048]{1,0:T(8,128)(2,1)} %get-tuple-element.84.refs_2_), custom_call_target="tpu_custom_call" | custom-call | flops 8053063680 | bytes 16777216 | tf_op jit(solution)/shard_map/cond/branch_1_fun/pallas_call | solution.py:199
  49.1 0.0 copy-start.4
  49.1 3.8 %all-to-all-done.2.refs_3_ = bf16[32,64,384]{2,1,0:T(8,128)(2,1)} async-done(((bf16[32,64,384]{2,1,0:T(8,128)(2,1)}), bf16[32,64,384]{2,1,0:T(8,128)(2,1)}, u32[]{:S(2)}, u32[]{:S(2)}) %all-to-all-start.2) | async-done | bytes 1572896 | tf_op jit(solution)/shard_map/cond/branch_1_fun/all_to_all | solution.py:340
  52.9 4.1 %all-to-all-start.3 = ((bf16[32,64,640]{2,1,0:T(8,128)(2,1)}), bf16[32,64,640]{2,1,0:T(8,128)(2,1)S(1)}, u32[]{:S(2)}, u32[]{:S(2)}) async-start(bf16[32,64,640]{2,1,0:T(8,128)(2,1)} %branch_1_fun.4), calls=%async_computation.3 | async-start | bytes 5242880 | tf_op jit(solution)/shard_map/cond/branch_1_fun/all_to_all | solution.py:344
  56.9 3.7 %collective-permute-start.1 = (bf16[32,64,384]{2,1,0:T(8,128)(2,1)}, bf16[32,64,384]{2,1,0:T(8,128)(2,1)}, u32[]{:S(2)}, u32[]{:S(2)}) collective-permute-start(bf16[32,64,384]{2,1,0:T(8,128)(2,1)} %all-to-all-done.2.refs_3_), channel_id=1, source_target_pairs={{1,0},{2,1},{3,2},{5,4},{6,5},{7,6},{9,8},{10,9},{11,10},{13,12},{... | collective-permute-start | bytes 4718600 | tf_op jit(solution)/shard_map/cond/branch_1_fun/ppermute | solution.py:343
  60.6 35.0 %collective-permute-done.1.refs_5_ = bf16[32,64,384]{2,1,0:T(8,128)(2,1)} collective-permute-done((bf16[32,64,384]{2,1,0:T(8,128)(2,1)}, bf16[32,64,384]{2,1,0:T(8,128)(2,1)}, u32[]{:S(2)}, u32[]{:S(2)}) %collective-permute-start.1) | collective-permute-done | bytes 1572896 | tf_op jit(solution)/shard_map/cond/branch_1_fun/ppermute | solution.py:343
  95.6 0.0 all-to-all-done.3.refs_4_
  95.6 0.0 copy-start.2
  95.6 1.5 %copy-done.2 = bf16[32,64,640]{2,1,0:T(8,128)(2,1)} copy-done((bf16[32,64,640]{2,1,0:T(8,128)(2,1)}, bf16[32,64,640]{2,1,0:T(8,128)(2,1)S(1)}, u32[]{:S(2)}) %copy-start.2) | copy-done | bytes 2621464 | tf_op jit(solution)/shard_map/cond
  97.1 0.0 copy-done.4
  97.1 14.2 %branch_1_fun.5 = bf16[4,32,2,128,128]{4,3,2,1,0:T(8,128)(2,1)} custom-call(s32[8,128]{1,0:T(8,128)S(1)} %get-tuple-element.79.refs_0_, s32[8,128]{1,0:T(8,128)S(1)} %get-tuple-element.80.refs_1_, bf16[256,256]{1,0:T(8,128)(2,1)S(1)} %copy-done.4, bf16[32,64,384]{2,1,0:T(8,128)(2,1)} %all-to-all-done.2.refs_3_, bf16[32,64,640]{2,1,0:T(8,128)(2,1)} %copy-done.2, ...), custom_call_target="tpu_custom_call" | custom-call | flops 3623878656 | bytes 14155776 | tf_op jit(solution)/shard_map/cond/branch_1_fun/pallas_call | solution.py:291
Async XLA Ops:
  1.4 6.7 %copy-start.9 = (s32[16,128]{1,0:T(8,128)}, s32[16,128]{1,0:T(8,128)S(1)}, u32[]{:S(2)}) copy-start(s32[16,128]{1,0:T(8,128)S(1)} %pad_add_fusion.refs_1_) | copy-start | bytes 24580
  1.4 4.8 %collective-permute-start.7 = (s32[16,128]{1,0:T(8,128)S(1)}, s32[16,128]{1,0:T(8,128)S(1)}, u32[]{:S(2)}, u32[]{:S(2)}) collective-permute-start(s32[16,128]{1,0:T(8,128)S(1)} %pad_add_fusion.refs_1_), channel_id=1, source_target_pairs={{0,1},{1,2},{2,3},{3,0},{4,5},{5,6},{6,7},{7,4},{8,9},{9,10},{10,1... | collective-permute-start | bytes 24584 | tf_op jit(solution)/shard_map/ppermute | solution.py:330
  2.9 5.2 %collective-permute-start.6 = (s32[16,128]{1,0:T(8,128)S(1)}, s32[16,128]{1,0:T(8,128)S(1)}, u32[]{:S(2)}, u32[]{:S(2)}) collective-permute-start(s32[16,128]{1,0:T(8,128)S(1)} %pad_add_fusion.refs_1_), channel_id=1, source_target_pairs={{0,2},{1,3},{2,0},{3,1},{4,6},{5,7},{6,4},{7,5},{8,10},{9,11},{10,... | collective-permute-start | bytes 24584 | tf_op jit(solution)/shard_map/ppermute | solution.py:330
  4.0 4.1 %collective-permute-start.5 = (s32[16,128]{1,0:T(8,128)S(1)}, s32[16,128]{1,0:T(8,128)S(1)}, u32[]{:S(2)}, u32[]{:S(2)}) collective-permute-start(s32[16,128]{1,0:T(8,128)S(1)} %pad_add_fusion.refs_1_), channel_id=1, source_target_pairs={{0,3},{1,0},{2,1},{3,2},{4,7},{5,4},{6,5},{7,6},{8,11},{9,8},{10,9... | collective-permute-start | bytes 24584 | tf_op jit(solution)/shard_map/ppermute | solution.py:330
  6.2 1.9 %copy-start.10 = (s32[16,128]{1,0:T(8,128)}, s32[16,128]{1,0:T(8,128)S(1)}, u32[]{:S(2)}) copy-start(s32[16,128]{1,0:T(8,128)S(1)} %collective-permute-done.7.refs_4_) | copy-start | bytes 24580
  8.1 0.6 copy-start.11
  8.1 0.6 copy-start.12
  21.7 31.2 %all-to-all-start.2 = ((bf16[32,64,384]{2,1,0:T(8,128)(2,1)}), bf16[32,64,384]{2,1,0:T(8,128)(2,1)}, u32[]{:S(2)}, u32[]{:S(2)}) async-start(bf16[32,64,384]{2,1,0:T(8,128)(2,1)} %branch_1_fun.3), calls=%async_computation.2 | async-start | bytes 3145728 | tf_op jit(solution)/shard_map/cond/branch_1_fun/all_to_all | solution.py:340
  49.1 48.1 %copy-start.4 = (bf16[256,256]{1,0:T(8,128)(2,1)S(1)}, bf16[256,256]{1,0:T(8,128)(2,1)}, u32[]{:S(2)}) copy-start(bf16[256,256]{1,0:T(8,128)(2,1)} %get-tuple-element.81.refs_2_) | copy-start | bytes 393220 | tf_op jit(solution)/shard_map/cond
  52.9 42.8 %all-to-all-start.3 = ((bf16[32,64,640]{2,1,0:T(8,128)(2,1)}), bf16[32,64,640]{2,1,0:T(8,128)(2,1)S(1)}, u32[]{:S(2)}, u32[]{:S(2)}) async-start(bf16[32,64,640]{2,1,0:T(8,128)(2,1)} %branch_1_fun.4), calls=%async_computation.3 | async-start | bytes 5242880 | tf_op jit(solution)/shard_map/cond/branch_1_fun/all_to_all | solution.py:344
  56.9 38.7 %collective-permute-start.1 = (bf16[32,64,384]{2,1,0:T(8,128)(2,1)}, bf16[32,64,384]{2,1,0:T(8,128)(2,1)}, u32[]{:S(2)}, u32[]{:S(2)}) collective-permute-start(bf16[32,64,384]{2,1,0:T(8,128)(2,1)} %all-to-all-done.2.refs_3_), channel_id=1, source_target_pairs={{1,0},{2,1},{3,2},{5,4},{6,5},{7,6},{9,8},{10,9},{11,10},{13,12},{... | collective-permute-start | bytes 4718600 | tf_op jit(solution)/shard_map/cond/branch_1_fun/ppermute | solution.py:343
  95.6 1.5 %copy-start.2 = (bf16[32,64,640]{2,1,0:T(8,128)(2,1)}, bf16[32,64,640]{2,1,0:T(8,128)(2,1)S(1)}, u32[]{:S(2)}) copy-start(bf16[32,64,640]{2,1,0:T(8,128)(2,1)S(1)} %all-to-all-done.3.refs_4_) | copy-start | bytes 7864324 | tf_op jit(solution)/shard_map/cond
